TPU v7x, 32 devices: a whole 2x2x4 slice. The times are simulated.
32 devices in a mesh: row: 4 (over y, x), col: 8 (over z, core).
Axes of the slice: x: 2, y: 2, z: 4, core: 2. Of those that a mesh axis runs over, the one named last changes fastest.
Arguments:
- tiles: bfloat16 [256, 256, 256], P(('row', 'col')), may hold values from -0.09375 to 0.09375
- tile_rows: int32 [256], P(('row', 'col')), may hold values from 0 to 3, as said below
- tile_cols: int32 [256], P(('row', 'col')), may hold values from 0 to 1
- tile_count: int32 [32], P(('row', 'col')), may hold values from 0 to 8, as said below
- bounds: float32 [2], replicated, may hold values from -1 to 2, as said below
- vectors: float32 [4096, 128], P(('row', 'col')), may hold values from -6 to 6
Outputs:
- filtered: float32 [4096, 128], P(('row', 'col'))
- gram: float32 [128, 128], replicated
Inputs may be any that keep to these rules, and one draw needn't show every extreme that they name: `tile_rows`: within each device the first tile_count slots name distinct blocks with global block row I <= global block column J; the device's diagonal blocks (I = J) come first; every diagonal block of the Hamiltonian is stored; slots after the live ones hold valid indices but are not part of the matrix. `tile_count`: devices whose block rows all lie below their block columns have no live slot; some device has all 8 slots live. bounds[0] < -0.5 and bounds[1] > 1.0.
All inputs are finite; a program needn't handle non-finite values.
Results may differ from a plain program's by a relative error of at most 0.0037.
Values may be sent and summed in bfloat16 or wider, within the bound.
A program may use at most 64 MiB of HBM per device.

v0:
```python
import jax
import jax.numpy as jnp
from jax import lax
from jax.sharding import PartitionSpec as P

BLK_COL = 2


def spread(block, axis, holder):
    block = jnp.where(lax.axis_index(axis) == holder, block, jnp.zeros_like(block))
    return lax.psum(block, axis)


def on_device(tiles, tile_rows, tile_cols, tile_count, bounds, vectors):
    col_ratio = lax.axis_size("col") // lax.axis_size("row")
    col_index = lax.axis_index("col")
    row_index = lax.axis_index("row")
    root_row = col_index // col_ratio
    slot_total = tiles.shape[0]
    block_size = tiles.shape[1]
    share_rows = vectors.shape[0]
    width_vecs = vectors.shape[1]
    group_rows = share_rows * lax.axis_size("col")
    group_blocks = group_rows // block_size
    column_rows = BLK_COL * block_size
    total_rows = share_rows * lax.axis_size("row") * lax.axis_size("col")
    offset = col_index % col_ratio * column_rows
    live_mask = (jnp.arange(slot_total, dtype=jnp.int32) < tile_count[0]).astype(jnp.bfloat16)
    owner_flag = (row_index == root_row).astype(jnp.float32)
    center = (bounds[1] + bounds[0]) * 0.5
    halfwidth = (bounds[1] - bounds[0]) * 0.5

    def apply_hamiltonian(current_vec):
        vector_panel = current_vec.astype(jnp.bfloat16)
        row_panel = lax.all_gather(vector_panel, "col", axis=0, tiled=True)
        col_piece = lax.dynamic_slice_in_dim(row_panel, offset, column_rows, 0)
        col_panel = spread(col_piece, "row", root_row)
        row_input = row_panel.reshape(group_blocks, block_size, width_vecs)
        col_input = col_panel.reshape(BLK_COL, block_size, width_vecs)
        start_rows = jnp.zeros((group_blocks, block_size, width_vecs), jnp.float32)
        start_cols = jnp.zeros((BLK_COL, block_size, width_vecs), jnp.float32)
        masked_cols = col_input[tile_cols] * live_mask[:, None, None]
        masked_rows = row_input[tile_rows] * live_mask[:, None, None]
        forward = jnp.einsum("tab,tbk->tak", tiles, masked_cols, preferred_element_type=jnp.float32)
        backward = jnp.einsum(
            "tab,tak->tbk", tiles, masked_rows, preferred_element_type=jnp.float32
        )
        row_part = start_rows.at[tile_rows].add(forward)
        col_part = start_cols.at[tile_cols].add(backward)
        column_total = lax.psum(col_part, "row")
        row_part = row_part.reshape(group_rows, width_vecs)
        present = lax.dynamic_slice_in_dim(row_part, offset, column_rows, 0)
        updated = present + owner_flag * column_total.reshape(column_rows, width_vecs)
        row_part = lax.dynamic_update_slice_in_dim(row_part, updated, offset, 0)
        return lax.psum_scatter(row_part, "col", scatter_dimension=0, tiled=True)

    current_vec = (apply_hamiltonian(vectors) - center * vectors) / halfwidth
    image = apply_hamiltonian(current_vec)
    following = 2.0 * (image - center * current_vec) / halfwidth - vectors
    current_vec = following
    gram_local = lax.dot_general(
        current_vec,
        current_vec,
        (((0,), (0,)), ((), ())),
        precision=lax.Precision.HIGHEST,
        preferred_element_type=jnp.float32,
    )
    gram_total = lax.psum(gram_local, ("row", "col"))
    return (current_vec, gram_total / total_rows)


def solution(mesh):
    in_specs = (
        P(("row", "col"), None, None),
        P(("row", "col")),
        P(("row", "col")),
        P(("row", "col")),
        P(),
        P(("row", "col"), None),
    )
    out_specs = (P(("row", "col"), None), P())
    return jax.shard_map(
        on_device, mesh=mesh, in_specs=in_specs, out_specs=out_specs, check_vma=False
    )
```

profile of v0, /device:TPU:1, one launch (start us, length us, event | category | flops | bytes accessed | tf_op | source)
XLA Modules:
  0.0 414.4 jit_solution(1064199134010569408)
XLA Ops:
  7.2 0.9 convert_element_type.16
  8.2 15.8 %all_gather.6 = bf16[1024,128]{1,0:T(8,128)(2,1)S(1)} all-gather(bf16[128,128]{1,0:T(8,128)(2,1)S(1)} %convert_element_type.16), channel_id=1, replica_groups=mesh['row'=4,'col'=8] {'col'}, dimensions={0}, use_global_device_ids=true | all-gather | bytes 294912 | tf_op jit(solution)/shard_map/all_gather | solution.py:35
  23.9 0.7 dynamic-slice_select_fusion.1
  24.6 0.0 all-reduce.8.cloned.1.call-start
  25.4 0.6 copy-done.9
  26.0 0.6 gather_fusion.1
  26.7 0.4 convolution_bitcast_fusion.2
  27.1 0.3 copy.15
  27.4 0.3 copy-done.10
  27.8 1.3 scatter_fusion.1
  29.1 0.7 copy-done.4
  29.8 0.0 reduce-scatter.3.cloned.1.call-start
  29.9 37.0 %all-reduce.6.cloned.1.call-done = bf16[2,256,128]{2,1,0:T(8,128)(2,1)} async-done(((bf16[2,256,128]{2,1,0:T(8,128)(2,1)}), bf16[2,256,128]{2,1,0:T(8,128)(2,1)}) %all-reduce.6.cloned.1.call-update) | async-done | bytes 131088 | tf_op jit(solution)/shard_map/psum | solution.py:11
  66.9 1.5 gather_fusion
  68.5 1.7 convolution_bitcast_fusion.3
  70.2 1.5 copy.13
  71.8 1.3 scatter_fusion
  73.1 39.9 %all-reduce.8.cloned.1.call-done = f32[2,256,128]{2,1,0:T(8,128)} async-done(((f32[2,256,128]{2,1,0:T(8,128)}), f32[2,256,128]{2,1,0:T(8,128)}) %all-reduce.8.cloned.1.call-update) | async-done | bytes 262160 | tf_op jit(solution)/shard_map/psum | solution.py:50
  113.1 1.0 broadcast_multiply_fusion.1
  114.0 0.1 constant_dynamic-update-slice_fusion.1
  114.1 0.8 copy-done.2
  114.9 0.0 all-reduce.10.cloned.1.call-start
  114.9 0.6 fusion.9
  118.1 25.2 %reduce-scatter.3.cloned.1.call-done = f32[128,128]{1,0:T(8,128)} async-done(((f32[1024,128]{1,0:T(8,128)}), f32[128,128]{1,0:T(8,128)}) %reduce-scatter.3.cloned.1.call-update) | async-done | bytes 65552 | tf_op jit(solution)/shard_map/reduce_scatter | solution.py:55
  143.4 0.9 fusion.8
  144.2 18.0 %all_gather.7 = bf16[1024,128]{1,0:T(8,128)(2,1)S(1)} all-gather(bf16[128,128]{1,0:T(8,128)(2,1)S(1)} %fusion.8), channel_id=1, replica_groups=mesh['row'=4,'col'=8] {'col'}, dimensions={0}, use_global_device_ids=true | all-gather | bytes 294912 | tf_op jit(solution)/shard_map/all_gather | solution.py:35
  162.3 0.7 dynamic-slice_select_fusion
  162.9 0.6 gather_fusion.3
  163.6 0.0 all-reduce.12.cloned.1.call-start
  163.7 0.4 convolution_bitcast_fusion
  164.1 0.3 copy.19
  164.4 1.3 scatter_fusion.3
  165.8 0.7 copy-done.3
  166.5 0.0 reduce-scatter.5.cloned.1.call-start
  166.6 36.5 %all-reduce.10.cloned.1.call-done = bf16[2,256,128]{2,1,0:T(8,128)(2,1)} async-done(((bf16[2,256,128]{2,1,0:T(8,128)(2,1)}), bf16[2,256,128]{2,1,0:T(8,128)(2,1)}) %all-reduce.10.cloned.1.call-update) | async-done | bytes 131088 | tf_op jit(solution)/shard_map/psum | solution.py:11
  203.1 1.5 gather_fusion.2
  204.7 1.7 convolution_bitcast_fusion.1
  206.4 1.5 copy.17
  208.0 1.3 scatter_fusion.2
  209.3 39.5 %all-reduce.12.cloned.1.call-done = f32[2,256,128]{2,1,0:T(8,128)} async-done(((f32[2,256,128]{2,1,0:T(8,128)}), f32[2,256,128]{2,1,0:T(8,128)}) %all-reduce.12.cloned.1.call-update) | async-done | bytes 262160 | tf_op jit(solution)/shard_map/psum | solution.py:50
  248.8 1.0 broadcast_multiply_fusion
  249.8 0.1 constant_dynamic-update-slice_fusion
  249.9 0.8 copy-done.1
  250.7 28.2 %reduce-scatter.5.cloned.1.call-done = f32[128,128]{1,0:T(8,128)} async-done(((f32[1024,128]{1,0:T(8,128)}), f32[128,128]{1,0:T(8,128)}) %reduce-scatter.5.cloned.1.call-update) | async-done | bytes 65552 | tf_op jit(solution)/shard_map/reduce_scatter | solution.py:55
  278.9 0.9 divide_subtract_fusion
  279.8 0.9 fusion.10
  280.8 125.3 %all-reduce.14.cloned.1.call-done = f32[128,128]{1,0:T(8,128)} async-done(((f32[128,128]{1,0:T(8,128)}), f32[128,128]{1,0:T(8,128)}) %all-reduce.14.cloned.1.call-update) | async-done | bytes 65552 | tf_op jit(solution)/shard_map/psum | solution.py:68
  406.1 1.5 broadcast_multiply_fusion.2
  (34 shorter events, 0.4 us)
Async XLA Ops:
  7.2 19.5 %copy-start = (bf16[8,256,256]{2,1,0:T(8,128)(2,1)S(1)}, bf16[8,256,256]{2,1,0:T(8,128)(2,1)}, u32[]{:S(2)}) copy-start(bf16[8,256,256]{2,1,0:T(8,128)(2,1)} %param.6) | copy-start | bytes 3145732
  7.2 59.8 %all-reduce.6.cloned.1.call-start = ((), (), s32[]{:S(2)}) async-start(), calls=%async_computation.2 | async-start | bytes 262144 | tf_op jit(solution)/shard_map/psum | solution.py:11
  24.6 88.4 %all-reduce.8.cloned.1.call-start = ((), (), s32[]{:S(2)}) async-start(), calls=%async_computation.3 | async-start | bytes 524288 | tf_op jit(solution)/shard_map/psum | solution.py:50
  25.3 0.7 copy-start.9
  27.1 0.7 copy-start.10
  29.1 0.7 copy-start.4
  29.8 113.5 %reduce-scatter.3.cloned.1.call-start = ((), (), s32[]{:S(2)}) async-start(), calls=%async_computation.4 | async-start | bytes 589824 | tf_op jit(solution)/shard_map/reduce_scatter | solution.py:55
  114.1 0.8 copy-start.2
  114.1 0.9 copy-start.8
  114.1 29.3 %copy-start.5 = (f32[128,128]{1,0:T(8,128)S(1)}, f32[128,128]{1,0:T(8,128)}, u32[]{:S(2)}) copy-start(f32[128,128]{1,0:T(8,128)} %param.11) | copy-start | bytes 196612
  114.9 88.2 %all-reduce.10.cloned.1.call-start = ((), (), s32[]{:S(2)}) async-start(), calls=%async_computation.5 | async-start | bytes 262144 | tf_op jit(solution)/shard_map/psum | solution.py:11
  163.6 85.2 %all-reduce.12.cloned.1.call-start = ((), (), s32[]{:S(2)}) async-start(), calls=%async_computation.6 | async-start | bytes 524288 | tf_op jit(solution)/shard_map/psum | solution.py:50
  165.8 0.7 copy-start.3
  166.5 112.4 %reduce-scatter.5.cloned.1.call-start = ((), (), s32[]{:S(2)}) async-start(), calls=%async_computation.7 | async-start | bytes 589824 | tf_op jit(solution)/shard_map/reduce_scatter | solution.py:55
  249.9 0.8 copy-start.1
  249.9 29.1 %copy-start.7 = (f32[128,128]{1,0:T(8,128)S(1)}, f32[128,128]{1,0:T(8,128)}, u32[]{:S(2)}) copy-start(f32[128,128]{1,0:T(8,128)} %reduce-scatter.3.cloned.1.call-done) | copy-start | bytes 196612
  250.7 155.4 %all-reduce.14.cloned.1.call-start = ((), (), s32[]{:S(2)}) async-start(), calls=%async_computation.8 | async-start | bytes 131072 | tf_op jit(solution)/shard_map/psum | solution.py:68
  279.8 0.9 copy-start.6
Sparse Core Ops, SparseCore 0:
  24.8 42.1 all-reduce.5
  70.1 42.8 all-reduce.7
  115.3 28.0 reduce-scatter.2
  163.7 39.3 all-reduce.9
  205.9 42.9 all-reduce.11
  251.0 27.8 reduce-scatter.4
  285.1 120.9 all-reduce.13
where the time goes:
time: 415 us; the launch traced here: 414 us
  waiting for transfers between devices  332 us (80%)
  blocking collectives  33.8 us (8%)
  between operations  17.7 us (4%)
  local copies, waits for them, and re-layouts  12.8 us (3%)
  other arithmetic  12.8 us (3%)
  matrix products  5.15 us (1%)
    psum x1, waiting for transfers between devices, on_device(): gram_total = lax.psum(gram_local, ('row', 'col'))  125 us
    psum x2, waiting for transfers between devices, apply_hamiltonian(): column_total = lax.psum(col_part, 'row')  79.5 us
    psum x2, waiting for transfers between devices, spread(): return lax.psum(block, axis)  73.6 us
    reduce_scatter x2, waiting for transfers between devices, apply_hamiltonian(): return lax.psum_scatter(row_part, 'col', scatter_dimension=0, tiled=True)  53.5 us
    all_gather x2, blocking collectives, apply_hamiltonian(): row_panel = lax.all_gather(vector_panel, 'col', axis=0, tiled=True)  33.8 us
  transfers between devices with their start and end apart: 7, of which 7 were waited for; matrix products, arithmetic and copies ran while one was open for 4% of the time, Pallas kernels for 0%

commit v1 on v0

--- a/solution.py
+++ b/solution.py
@@ -65,7 +65,7 @@
         precision=lax.Precision.HIGHEST,
         preferred_element_type=jnp.float32,
     )
-    gram_total = lax.psum(gram_local, ("row", "col"))
+    gram_total = lax.psum(lax.psum(gram_local, "col"), "row")
     return (current_vec, gram_total / total_rows)
 
 

time: 415 us -> 390 us (0.940)
  waiting for transfers between devices: 332 us -> 306 us
    psum x1 -> x2, waiting for transfers between devices: 125 us -> 99.6 us  [on_device(): gram_total = lax.psum(lax.psum(gram_local, 'col'), 'row')]
  transfers between devices with their start and end apart: 7 -> 8, of which waited for: 7 -> 8; matrix products, arithmetic and copies ran while one was open for 4% -> 5% of each run, Pallas kernels for 0% -> 0%
where the time goes in v1:
time: 390 us; the launch traced here: 389 us
  waiting for transfers between devices  306 us (78%)
  blocking collectives  33.8 us (9%)
  between operations  17.7 us (5%)
  local copies, waits for them, and re-layouts  12.8 us (3%)
  other arithmetic  12.8 us (3%)
  matrix products  5.15 us (1%)
    psum x2, waiting for transfers between devices, on_device(): gram_total = lax.psum(lax.psum(gram_local, 'col'), 'row')  99.6 us
    psum x2, waiting for transfers between devices, apply_hamiltonian(): column_total = lax.psum(col_part, 'row')  79.5 us
    psum x2, waiting for transfers between devices, spread(): return lax.psum(block, axis)  73.6 us
    reduce_scatter x2, waiting for transfers between devices, apply_hamiltonian(): return lax.psum_scatter(row_part, 'col', scatter_dimension=0, tiled=True)  53.5 us
    all_gather x2, blocking collectives, apply_hamiltonian(): row_panel = lax.all_gather(vector_panel, 'col', axis=0, tiled=True)  33.8 us
  transfers between devices with their start and end apart: 8, of which 8 were waited for; matrix products, arithmetic and copies ran while one was open for 5% of the time, Pallas kernels for 0%

profile of v1, /device:TPU:1, one launch (start us, length us, event | category | flops | bytes accessed | tf_op | source)
XLA Modules:
  0.0 388.7 jit_solution(13589876530114365089)
XLA Ops:
  7.2 0.9 convert_element_type.16
  8.2 15.8 %all_gather.6 = bf16[1024,128]{1,0:T(8,128)(2,1)S(1)} all-gather(bf16[128,128]{1,0:T(8,128)(2,1)S(1)} %convert_element_type.16), channel_id=1, replica_groups=mesh['row'=4,'col'=8] {'col'}, dimensions={0}, use_global_device_ids=true | all-gather | bytes 294912 | tf_op jit(solution)/shard_map/all_gather | solution.py:35
  23.9 0.7 dynamic-slice_select_fusion.1
  24.6 0.0 all-reduce.9.cloned.1.call-start
  25.4 0.6 copy-done.9
  26.0 0.6 gather_fusion.1
  26.7 0.4 convolution_bitcast_fusion.2
  27.1 0.3 copy.15
  27.4 0.3 copy-done.10
  27.8 1.3 scatter_fusion.1
  29.1 0.7 copy-done.4
  29.8 0.0 reduce-scatter.3.cloned.1.call-start
  29.9 37.0 %all-reduce.7.cloned.1.call-done = bf16[2,256,128]{2,1,0:T(8,128)(2,1)} async-done(((bf16[2,256,128]{2,1,0:T(8,128)(2,1)}), bf16[2,256,128]{2,1,0:T(8,128)(2,1)}) %all-reduce.7.cloned.1.call-update) | async-done | bytes 131088 | tf_op jit(solution)/shard_map/psum | solution.py:11
  66.9 1.5 gather_fusion
  68.5 1.7 convolution_bitcast_fusion.3
  70.2 1.5 copy.13
  71.8 1.3 scatter_fusion
  73.1 39.9 %all-reduce.9.cloned.1.call-done = f32[2,256,128]{2,1,0:T(8,128)} async-done(((f32[2,256,128]{2,1,0:T(8,128)}), f32[2,256,128]{2,1,0:T(8,128)}) %all-reduce.9.cloned.1.call-update) | async-done | bytes 262160 | tf_op jit(solution)/shard_map/psum | solution.py:50
  113.1 1.0 broadcast_multiply_fusion.1
  114.0 0.1 constant_dynamic-update-slice_fusion.1
  114.1 0.8 copy-done.2
  114.9 0.0 all-reduce.11.cloned.1.call-start
  114.9 0.6 fusion.9
  118.1 25.2 %reduce-scatter.3.cloned.1.call-done = f32[128,128]{1,0:T(8,128)} async-done(((f32[1024,128]{1,0:T(8,128)}), f32[128,128]{1,0:T(8,128)}) %reduce-scatter.3.cloned.1.call-update) | async-done | bytes 65552 | tf_op jit(solution)/shard_map/reduce_scatter | solution.py:55
  143.4 0.9 fusion.8
  144.2 18.0 %all_gather.7 = bf16[1024,128]{1,0:T(8,128)(2,1)S(1)} all-gather(bf16[128,128]{1,0:T(8,128)(2,1)S(1)} %fusion.8), channel_id=1, replica_groups=mesh['row'=4,'col'=8] {'col'}, dimensions={0}, use_global_device_ids=true | all-gather | bytes 294912 | tf_op jit(solution)/shard_map/all_gather | solution.py:35
  162.3 0.7 dynamic-slice_select_fusion
  162.9 0.6 gather_fusion.3
  163.7 0.4 convolution_bitcast_fusion
  164.1 0.3 copy.19
  164.4 1.3 scatter_fusion.3
  165.8 0.7 copy-done.3
  166.5 0.0 reduce-scatter.5.cloned.1.call-start
  166.6 36.5 %all-reduce.11.cloned.1.call-done = bf16[2,256,128]{2,1,0:T(8,128)(2,1)} async-done(((bf16[2,256,128]{2,1,0:T(8,128)(2,1)}), bf16[2,256,128]{2,1,0:T(8,128)(2,1)}) %all-reduce.11.cloned.1.call-update) | async-done | bytes 131088 | tf_op jit(solution)/shard_map/psum | solution.py:11
  203.1 1.5 gather_fusion.2
  204.7 1.7 convolution_bitcast_fusion.1
  206.4 1.5 copy.17
  208.0 1.3 scatter_fusion.2
  209.3 39.5 %all-reduce.13.cloned.1.call-done = f32[2,256,128]{2,1,0:T(8,128)} async-done(((f32[2,256,128]{2,1,0:T(8,128)}), f32[2,256,128]{2,1,0:T(8,128)}) %all-reduce.13.cloned.1.call-update) | async-done | bytes 262160 | tf_op jit(solution)/shard_map/psum | solution.py:50
  248.8 1.0 broadcast_multiply_fusion
  249.8 0.1 constant_dynamic-update-slice_fusion
  249.9 0.8 copy-done.1
  250.7 28.2 %reduce-scatter.5.cloned.1.call-done = f32[128,128]{1,0:T(8,128)} async-done(((f32[1024,128]{1,0:T(8,128)}), f32[128,128]{1,0:T(8,128)}) %reduce-scatter.5.cloned.1.call-update) | async-done | bytes 65552 | tf_op jit(solution)/shard_map/reduce_scatter | solution.py:55
  278.9 0.9 divide_subtract_fusion
  279.8 0.9 fusion.10
  280.8 54.7 %all-reduce.15.cloned.1.call-done = f32[128,128]{1,0:T(8,128)} async-done(((f32[128,128]{1,0:T(8,128)}), f32[128,128]{1,0:T(8,128)}) %all-reduce.15.cloned.1.call-update) | async-done | bytes 65552 | tf_op jit(solution)/shard_map/psum | solution.py:68
  335.6 44.8 %all-reduce.17.cloned.1.call-done = f32[128,128]{1,0:T(8,128)} async-done(((f32[128,128]{1,0:T(8,128)}), f32[128,128]{1,0:T(8,128)}) %all-reduce.17.cloned.1.call-update) | async-done | bytes 65552 | tf_op jit(solution)/shard_map/psum | solution.py:68
  380.4 1.5 broadcast_multiply_fusion.2
  (37 shorter events, 0.5 us)
Async XLA Ops:
  7.2 19.5 %copy-start = (bf16[8,256,256]{2,1,0:T(8,128)(2,1)S(1)}, bf16[8,256,256]{2,1,0:T(8,128)(2,1)}, u32[]{:S(2)}) copy-start(bf16[8,256,256]{2,1,0:T(8,128)(2,1)} %param.6) | copy-start | bytes 3145732
  7.2 59.8 %all-reduce.7.cloned.1.call-start = ((), (), s32[]{:S(2)}) async-start(), calls=%async_computation.2 | async-start | bytes 262144 | tf_op jit(solution)/shard_map/psum | solution.py:11
  24.6 88.4 %all-reduce.9.cloned.1.call-start = ((), (), s32[]{:S(2)}) async-start(), calls=%async_computation.3 | async-start | bytes 524288 | tf_op jit(solution)/shard_map/psum | solution.py:50
  25.3 0.7 copy-start.9
  27.1 0.7 copy-start.10
  29.1 0.7 copy-start.4
  29.8 113.5 %reduce-scatter.3.cloned.1.call-start = ((), (), s32[]{:S(2)}) async-start(), calls=%async_computation.4 | async-start | bytes 589824 | tf_op jit(solution)/shard_map/reduce_scatter | solution.py:55
  114.1 0.8 copy-start.2
  114.1 0.9 copy-start.8
  114.1 29.3 %copy-start.5 = (f32[128,128]{1,0:T(8,128)S(1)}, f32[128,128]{1,0:T(8,128)}, u32[]{:S(2)}) copy-start(f32[128,128]{1,0:T(8,128)} %param.11) | copy-start | bytes 196612
  114.9 88.2 %all-reduce.11.cloned.1.call-start = ((), (), s32[]{:S(2)}) async-start(), calls=%async_computation.5 | async-start | bytes 262144 | tf_op jit(solution)/shard_map/psum | solution.py:11
  163.6 85.2 %all-reduce.13.cloned.1.call-start = ((), (), s32[]{:S(2)}) async-start(), calls=%async_computation.6 | async-start | bytes 524288 | tf_op jit(solution)/shard_map/psum | solution.py:50
  165.8 0.7 copy-start.3
  166.5 112.4 %reduce-scatter.5.cloned.1.call-start = ((), (), s32[]{:S(2)}) async-start(), calls=%async_computation.7 | async-start | bytes 589824 | tf_op jit(solution)/shard_map/reduce_scatter | solution.py:55
  249.9 0.8 copy-start.1
  249.9 29.1 %copy-start.7 = (f32[128,128]{1,0:T(8,128)S(1)}, f32[128,128]{1,0:T(8,128)}, u32[]{:S(2)}) copy-start(f32[128,128]{1,0:T(8,128)} %reduce-scatter.3.cloned.1.call-done) | copy-start | bytes 196612
  250.7 84.9 %all-reduce.15.cloned.1.call-start = ((), (), s32[]{:S(2)}) async-start(), calls=%async_computation.8 | async-start | bytes 131072 | tf_op jit(solution)/shard_map/psum | solution.py:68
  279.8 0.9 copy-start.6
  280.8 99.6 %all-reduce.17.cloned.1.call-start = ((), (), s32[]{:S(2)}) async-start(), calls=%async_computation.9 | async-start | bytes 131072 | tf_op jit(solution)/shard_map/psum | solution.py:68
Sparse Core Ops, SparseCore 0:
  24.8 42.1 all-reduce.6
  70.1 42.8 all-reduce.8
  115.3 28.0 reduce-scatter.2
  163.7 39.3 all-reduce.10
  205.9 42.9 all-reduce.12
  251.0 27.8 reduce-scatter.4
  281.8 53.6 all-reduce.14
  338.7 41.6 all-reduce.16
